TPU v7x, 256 devices: a whole 4x4x8 slice. The times are simulated.
256 devices in a mesh: hid: 4 (over x), src: 32 (over z, y), tgt: 2 (over core).
Axes of the slice: x: 4, y: 4, z: 8, core: 2. Of those that a mesh axis runs over, the one named last changes fastest.
Arguments:
- decoder_slab: float32 [65536, 3584], P('src', 'hid'), may hold values from -1000 to 1000, as said below
- encoder_panel: float32 [3584, 1024], P(('hid', 'src'), 'tgt'), may hold values from -6 to 6
Outputs:
- virtual: float32 [65536, 2, 512], P('src', 'tgt', 'hid')
Inputs may be any that keep to these rules, and one draw needn't show every extreme that they name: `decoder_slab`: float32 decoder rows.
All inputs are finite; a program needn't handle non-finite values.
Results may differ from a plain program's by a relative error of at most 0.000071.
Values sent between devices are 32-bit elements; how exact they have to be, the bound alone decides.
A program may use at most 128 MiB of HBM per device.

v0:
```python
import jax
import jax.numpy as jnp
from jax import lax
from jax.sharding import PartitionSpec as P

EPS = 1e-06


def summed_inverse(squares):
    total = lax.psum(squares, "hid")
    return lax.rsqrt(total + EPS)


def make_adder(left, piece):
    return jnp.dot(left, piece, precision=lax.Precision.HIGHEST, preferred_element_type=jnp.float32)


def shards(decoder_slab, encoder_panel):
    rows = decoder_slab.shape[0]
    squares = jnp.sum(decoder_slab * decoder_slab, axis=1, keepdims=True)
    inverse = summed_inverse(squares)
    left = decoder_slab * inverse
    partial_value = make_adder(left, lax.all_gather(encoder_panel, "src", axis=0, tiled=True))
    share = lax.psum_scatter(partial_value, "hid", scatter_dimension=1, tiled=True)
    return share.reshape(rows, 1, share.shape[1])


def solution(mesh):
    placed = (P("src", "hid"), P(("hid", "src"), "tgt"))
    return jax.shard_map(
        shards, mesh=mesh, in_specs=placed, out_specs=P("src", "tgt", "hid"), check_vma=False
    )
```

profile of v0, /device:TPU:2, one launch (start us, length us, event | category | flops | bytes accessed | tf_op | source)
XLA Modules:
  0.0 161.6 jit_solution(14249240245569041440)
XLA Ops:
  6.5 0.0 all-gather.3.cloned.1.call-start
  6.5 0.7 all-gather.3.cloned.1.call-update
  7.3 0.0 reduce-scatter.2.cloned.1.call-start
  7.3 3.6 %multiply_reduce_fusion = f32[2048]{0:T(1024)S(1)} fusion(f32[2048,896]{1,0:T(8,128)} %param.2), kind=kLoop, calls=%fused_computation.2 | loop fusion | flops 3667968 | bytes 7348224 | tf_op jit(solution)/shard_map/reduce_sum | solution.py:20
  10.9 10.1 %psum.7 = f32[2048,1]{0,1:T(1,128)S(1)} all-reduce(f32[2048,1]{0,1:T(1,128)S(1)} %bitcast.9), channel_id=1, replica_groups=mesh['hid'=4,'src'=32,'tgt'=2] {'hid'}, use_global_device_ids=true, to_apply=%region_1.0 | all-reduce | flops 2048 | bytes 16384 | tf_op jit(solution)/shard_map/psum | solution.py:10
  21.1 69.9 %all-gather.3.cloned.1.call-done = f32[32,28,512]{2,1,0:T(8,128)} async-done(((f32[1,28,512]{2,1,0:T(8,128)}), f32[32,28,512]{2,1,0:T(8,128)}) %all-gather.3.cloned.1.call-update) | async-done | bytes 1835024 | tf_op jit(solution)/shard_map/all_gather | solution.py:23
  90.9 1.6 %reshape.5 = f32[896,512]{1,0:T(8,128)S(1)} reshape(f32[32,28,512]{2,1,0:T(8,128)} %all-gather.3.cloned.1.call-done) | data formatting | bytes 3670016
  92.6 16.8 %fusion = f32[2048,512]{1,0:T(8,128)} fusion(f32[896,512]{1,0:T(8,128)S(1)} %reshape.5, f32[2048,896]{1,0:T(8,128)} %param.2, f32[2048]{0:T(1024)S(1)} %bitcast.7), kind=kOutput, calls=%fused_computation | convolution fusion | flops 11276124160 | bytes 13377536 | tf_op jit(solution)/shard_map/dot_general | solution.py:15
  109.4 0.0 reduce-scatter.2.cloned.1.call-update
  109.4 45.4 %reduce-scatter.2.cloned.1.call-done = f32[2048,128]{1,0:T(8,128)} async-done(((f32[2048,512]{1,0:T(8,128)}), f32[2048,128]{1,0:T(8,128)}) %reduce-scatter.2.cloned.1.call-update) | async-done | bytes 1048592 | tf_op jit(solution)/shard_map/reduce_scatter | solution.py:24
  (1 shorter events, 0.0 us)
Async XLA Ops:
  6.5 84.4 %all-gather.3.cloned.1.call-start = ((), (), s32[]{:S(2)}) async-start(), calls=%async_computation.2 | async-start | bytes 2162688 | tf_op jit(solution)/shard_map/all_gather | solution.py:23
  7.3 147.5 %reduce-scatter.2.cloned.1.call-start = ((), (), s32[]{:S(2)}) async-start(), calls=%async_computation.1 | async-start | bytes 5242880 | tf_op jit(solution)/shard_map/reduce_scatter | solution.py:24
Sparse Core Ops, SparseCore 0:
  9.9 80.9 all-gather.2
  109.5 45.2 reduce-scatter.1
where the time goes:
time: 164 us; the launch traced here: 162 us
  waiting for transfers between devices  116 us (71%)
  matrix products  16.8 us (10%)
  between operations  13.4 us (8%)
  blocking collectives  10.1 us (6%)
  other arithmetic  3.65 us (2%)
    all_gather x1, waiting for transfers between devices, shards(): lax.all_gather(encoder_panel, 'src', axis=0, tiled=True)  69.9 us
    reduce_scatter x1, waiting for transfers between devices, shards(): lax.psum_scatter(partial_value, 'hid', scatter_dimension=1, tiled=True)  45.4 us
    dot_general x1, matrix products, make_adder(): jnp.dot(left, piece, precision=lax.Precision.HIGHEST, preferred_element_t...  16.8 us
    psum x1, blocking collectives, summed_inverse(): total = lax.psum(squares, 'hid')  10.1 us
    reduce_sum x1, other arithmetic, shards(): squares = jnp.sum(decoder_slab * decoder_slab, axis=1, keepdims=True)  3.63 us
  transfers between devices with their start and end apart: 2, of which 2 were waited for; matrix products, arithmetic and copies ran while one was open for 2% of the time, Pallas kernels for 0%

commit v1 on v0

v1 whole, which is shorter than its diff:
```python
import jax
import jax.numpy as jnp
from jax import lax
from jax.experimental import pallas as pl
from jax.experimental.pallas import tpu as pltpu
from jax.sharding import PartitionSpec as P

EPS = 1e-06
MESH = pl.DeviceIdType.MESH
NX, NY, NZ = 4, 4, 8
ROWS, K, W = 2048, 896, 128
HALF = ROWS // 2
SHARD = K // (NY * NZ)
DCH = 256
RB = 256
NB = HALF // RB
ZS = (4, 3, 5, 2, 6, 1, 7)
YS = (2, 1, 3)
XS = (2, 1, 3)
FAR, NEAR, SUM = 0, 1, 2
PLUS, MINUS = 0, 1


def kernel(d_ref, e_ref, o_ref, dbuf, ds, land, rhs, sq, sqin, out_x, in_x,
           dsem, esem, zss, zrs, yss, yrs, xss, xrs, qss, qrs):
    h = lax.axis_index("hid")
    s = lax.axis_index("src")
    z, y = s // NY, lax.rem(s, NY)

    def at_x(d):
        return {"hid": lax.rem(h + d, NX)}

    def at_z(d):
        return {"src": lax.rem(z + d, NZ) * NY + y}

    def at_y(d):
        return {"src": z * NY + lax.rem(y + d, NY)}

    def load(i):
        return pltpu.make_async_copy(
            d_ref.at[pl.ds(i * DCH, DCH)], dbuf.at[pl.ds(i * DCH, DCH)], dsem.at[i])

    def columns(u):
        t = lax.rem(h + u, NX)
        return e_ref.at[:, pl.ds(pl.multiple_of(t * W, W), W)]

    def own_piece(u):
        return pltpu.make_async_copy(columns(u), land.at[u, z, y], esem.at[u])

    def z_send(u, i):
        return pltpu.make_async_remote_copy(
            src_ref=columns(u), dst_ref=land.at[u, z, y], send_sem=zss.at[u, i], recv_sem=zrs.at[u, i],
            device_id=at_z(ZS[i]), device_id_type=MESH)

    def y_send(u, i, j):
        zz = z if i == NZ - 1 else lax.rem(z + NZ - ZS[i], NZ)
        return pltpu.make_async_remote_copy(
            src_ref=land.at[u, zz, y], dst_ref=land.at[u, zz, y], send_sem=yss.at[u, i, j],
            recv_sem=yrs.at[u, i, j], device_id=at_y(YS[j]), device_id_type=MESH)

    def sq_send(i):
        return pltpu.make_async_remote_copy(
            src_ref=sq, dst_ref=sqin.at[i], send_sem=qss.at[i], recv_sem=qrs.at[i],
            device_id=at_x(XS[i]), device_id_type=MESH)

    def x_send(part, way, b):
        return pltpu.make_async_remote_copy(
            src_ref=out_x.at[part, way, pl.ds(b * RB, RB)], dst_ref=in_x.at[part, way, pl.ds(b * RB, RB)],
            send_sem=xss.at[part, way, b], recv_sem=xrs.at[part, way, b],
            device_id=at_x(1 if way == PLUS else 3), device_id_type=MESH)

    def split(i):
        load(i).wait()
        d = dbuf[pl.ds(i * DCH, DCH), :]
        hi = d.astype(jnp.bfloat16)
        ds[pl.ds(i * DCH, DCH), 0:K] = hi
        ds[pl.ds(i * DCH, DCH), K:2 * K] = (d - hi.astype(jnp.float32)).astype(jnp.bfloat16)
        p = d[:, 0:W] * d[:, 0:W]
        for c in range(1, K // W):
            q = d[:, c * W:(c + 1) * W]
            p = p + q * q
        for c in range(DCH // W):
            row = jnp.sum(p[c * W:(c + 1) * W].T, axis=0, keepdims=True)
            sq[i * (DCH // W) + c:i * (DCH // W) + c + 1, :] = row

    def z_start(u):
        for i in range(NZ - 1):
            z_send(u, i).start()

    def y_start(u):
        own_piece(u).wait()
        for j in range(3):
            y_send(u, NZ - 1, j).start()
        for i in range(NZ - 1):
            z_send(u, i).wait_recv()
            for j in range(3):
                y_send(u, i, j).start()

    def y_wait(u):
        for i in range(NZ):
            for j in range(3):
                y_send(u, i, j).wait_recv()

    def panel(u):
        for a in range(NZ):
            for b in range(0, NY, 4):
                e = jnp.concatenate([land[u, a, b + k] for k in range(4)], axis=0)
                hi = e.astype(jnp.bfloat16)
                lo = (e - hi.astype(jnp.float32)).astype(jnp.bfloat16)
                r = (a * NY + b) * SHARD
                for off in (0, K):
                    rhs[u, off + r:off + r + 4 * SHARD, 0:W] = hi
                    rhs[u, off + r:off + r + 4 * SHARD, W:2 * W] = lo

    def product(u, r):
        full = jnp.dot(ds[pl.ds(r, RB), :], rhs[u], preferred_element_type=jnp.float32)
        return full[:, 0:W] + full[:, W:2 * W]

    for i in range(ROWS // DCH):
        load(i).start()
    for u in (2, 1, 3, 0):
        own_piece(u).start()
    barrier = pltpu.get_barrier_semaphore()
    for peer in [at_z(d) for d in ZS] + [at_y(d) for d in YS] + [at_x(d) for d in XS]:
        pl.semaphore_signal(barrier, inc=1, device_id=peer, device_id_type=MESH)
    pl.semaphore_wait(barrier, len(ZS) + len(YS) + len(XS))

    z_start(2)
    for i in range(0, 4):
        split(i)
    y_start(2)
    z_start(1)
    z_start(3)
    for i in range(4, 8):
        split(i)
    for i in range(3):
        sq_send(i).start()
    y_wait(2)
    panel(2)

    def far_block(b):
        for way, base in ((PLUS, HALF), (MINUS, 0)):
            out_x[FAR, way, pl.ds(b * RB, RB), :] = product(2, base + b * RB)
            x_send(FAR, way, b).start()

    for b in range(0, NB // 2):
        far_block(b)
    y_start(1)
    y_start(3)
    for b in range(NB // 2, NB):
        far_block(b)
    z_start(0)
    y_wait(1)
    panel(1)
    y_wait(3)
    panel(3)
    for b in range(NB):
        for way, base, u in ((PLUS, 0, 1), (MINUS, HALF, 3)):
            out_x[NEAR, way, pl.ds(b * RB, RB), :] = product(u, base + b * RB)
            x_send(NEAR, way, b).start()
    y_start(0)
    for b in range(NB):
        for way, base, u in ((PLUS, HALF, 1), (MINUS, 0, 3)):
            mine = product(u, base + b * RB)
            x_send(FAR, way, b).wait_recv()
            out_x[SUM, way, pl.ds(b * RB, RB), :] = mine + in_x[FAR, way, pl.ds(b * RB, RB), :]
            x_send(SUM, way, b).start()
    y_wait(0)
    panel(0)
    for b in range(ROWS // RB):
        o_ref[pl.ds(b * RB, RB), :] = product(0, b * RB)
    for i in range(3):
        sq_send(i).wait_recv()
    inverse = lax.rsqrt(sq[...] + sqin[0] + sqin[1] + sqin[2] + EPS)
    for b in range(NB):
        x_send(NEAR, PLUS, b).wait_recv()
        x_send(NEAR, MINUS, b).wait_recv()
        for way, base, near in ((PLUS, HALF, MINUS), (MINUS, 0, PLUS)):
            x_send(SUM, way, b).wait_recv()
            r = base + b * RB
            total = (o_ref[pl.ds(r, RB), :] + in_x[NEAR, near, pl.ds(b * RB, RB), :]
                     + in_x[SUM, way, pl.ds(b * RB, RB), :])
            for c in range(RB // W):
                i = r // W + c
                scale = jnp.broadcast_to(inverse[i:i + 1, :], (W, W)).T
                o_ref[pl.ds(r + c * W, W), :] = total[c * W:(c + 1) * W] * scale

    for u in range(NX):
        for i in range(NZ - 1):
            z_send(u, i).wait_send()
        for i in range(NZ):
            for j in range(3):
                y_send(u, i, j).wait_send()
    for i in range(3):
        sq_send(i).wait_send()
    for part in range(3):
        for way in range(2):
            for b in range(NB):
                x_send(part, way, b).wait_send()


def shards(decoder_slab, encoder_panel):
    f32, bf16 = jnp.float32, jnp.bfloat16
    dma = pltpu.SemaphoreType.DMA
    out = pl.pallas_call(
        kernel,
        out_shape=jax.ShapeDtypeStruct((ROWS, W), f32),
        in_specs=[pl.BlockSpec(memory_space=pl.ANY)] * 2,
        out_specs=pl.BlockSpec(memory_space=pltpu.VMEM),
        scratch_shapes=[
            pltpu.VMEM((ROWS, K), f32),
            pltpu.VMEM((ROWS, 2 * K), bf16),
            pltpu.VMEM((NX, NZ, NY, SHARD, W), f32),
            pltpu.VMEM((NX, 2 * K, 2 * W), bf16),
            pltpu.VMEM((ROWS // W, W), f32),
            pltpu.VMEM((3, ROWS // W, W), f32),
            pltpu.VMEM((3, 2, HALF, W), f32),
            pltpu.VMEM((3, 2, HALF, W), f32),
            dma((ROWS // DCH,)), dma((NX,)),
            dma((NX, NZ - 1)), dma((NX, NZ - 1)),
            dma((NX, NZ, 3)), dma((NX, NZ, 3)),
            dma((3, 2, NB)), dma((3, 2, NB)),
            dma((3,)), dma((3,)),
        ],
        compiler_params=pltpu.CompilerParams(
            collective_id=0, has_side_effects=True, vmem_limit_bytes=56 * 1024 * 1024),
    )(decoder_slab, encoder_panel)
    return out.reshape(ROWS, 1, W)


def solution(mesh):
    placed = (P("src", "hid"), P(("hid", "src"), "tgt"))
    return jax.shard_map(
        shards, mesh=mesh, in_specs=placed, out_specs=P("src", "tgt", "hid"), check_vma=False
    )
```

time: 164 us -> 61 us (0.37); the launches traced: 162 us -> 60.9 us
  waiting for transfers between devices: 116 us -> 0 us
  Pallas kernels: 0 us -> 58.8 us
  matrix products: 16.8 us -> 0 us
  between operations: 13.4 us -> 0.01 us
  blocking collectives: 10.1 us -> 0 us
  other arithmetic: 3.65 us -> 0 us
    all_gather x1 -> x0, waiting for transfers between devices: 69.9 us -> none  [shards(): lax.all_gather(encoder_panel, 'src', axis=0, tiled=True)]
    pallas_call x0 -> x1, Pallas kernels: none -> 58.8 us  [shards(): pl.pallas_call(kernel, out_shape=jax.ShapeDtypeStruct((ROWS, W), f32), in...]
    reduce_scatter x1 -> x0, waiting for transfers between devices: 45.4 us -> none  [shards(): lax.psum_scatter(partial_value, 'hid', scatter_dimension=1, tiled=True)]
    dot_general x1 -> x0, matrix products: 16.8 us -> none  [make_adder(): jnp.dot(left, piece, precision=lax.Precision.HIGHEST, preferred_element_t...]
    psum x1 -> x0, blocking collectives: 10.1 us -> none  [summed_inverse(): total = lax.psum(squares, 'hid')]
    reduce_sum x1 -> x0, other arithmetic: 3.63 us -> none  [shards(): squares = jnp.sum(decoder_slab * decoder_slab, axis=1, keepdims=True)]
  transfers between devices with their start and end apart: 2 -> 0, of which waited for: 2 -> 0; matrix products, arithmetic and copies ran while one was open for 2% -> 0% of each run, Pallas kernels for 0% -> 0%
where the time goes in v1:
time: 61 us; the launch traced here: 60.9 us
  Pallas kernels  58.8 us (96%)
  local copies, waits for them, and re-layouts  2.05 us (3%)
    pallas_call x1, Pallas kernels, shards(): pl.pallas_call(kernel, out_shape=jax.ShapeDtypeStruct((ROWS, W), f32), in...  58.8 us
    unnamed x1, local copies, waits for them, and re-layouts  2.05 us

profile of v1, /device:TPU:2, one launch (start us, length us, event | category | flops | bytes accessed | tf_op | source)
XLA Modules:
  0.0 60.9 jit_solution(17728247270346544303)
XLA Ops:
  0.0 58.8 %shard_map.28 = f32[2048,128]{1,0:T(8,128)} custom-call(f32[2048,896]{1,0:T(8,128)} %d_ref.1, f32[28,512]{1,0:T(8,128)} %e_ref.1), custom_call_target="tpu_custom_call" | custom-call | tf_op jit(solution)/shard_map/pallas_call | solution.py:205
  58.8 2.0 %copy.5 = f32[2048,1,128]{2,1,0:T(1,128)} copy(f32[2048,1,128]{2,1,0:T(1,128)} %bitcast.3) | data formatting | bytes 2097152

commit v2 on v1

--- a/solution.py
+++ b/solution.py
@@ -83,65 +83,81 @@
             row = jnp.sum(p[c * W:(c + 1) * W].T, axis=0, keepdims=True)
             sq[i * (DCH // W) + c:i * (DCH // W) + c + 1, :] = row
 
+    sent, due = [], {}
+
+    def go(make, *key):
+        copy = make(*key)
+        copy.start()
+        sent.append(copy)
+        due[(make,) + key] = copy
+
+    def got(make, *key):
+        due.pop((make,) + key).wait_recv()
+
     def z_start(u):
         for i in range(NZ - 1):
-            z_send(u, i).start()
+            go(z_send, u, i)
 
     def y_start(u):
         own_piece(u).wait()
         for j in range(3):
-            y_send(u, NZ - 1, j).start()
+            go(y_send, u, NZ - 1, j)
         for i in range(NZ - 1):
-            z_send(u, i).wait_recv()
+            got(z_send, u, i)
             for j in range(3):
-                y_send(u, i, j).start()
+                go(y_send, u, i, j)
 
     def y_wait(u):
         for i in range(NZ):
             for j in range(3):
-                y_send(u, i, j).wait_recv()
+                got(y_send, u, i, j)
 
     def panel(u):
         for a in range(NZ):
-            for b in range(0, NY, 4):
-                e = jnp.concatenate([land[u, a, b + k] for k in range(4)], axis=0)
-                hi = e.astype(jnp.bfloat16)
-                lo = (e - hi.astype(jnp.float32)).astype(jnp.bfloat16)
-                r = (a * NY + b) * SHARD
-                for off in (0, K):
-                    rhs[u, off + r:off + r + 4 * SHARD, 0:W] = hi
-                    rhs[u, off + r:off + r + 4 * SHARD, W:2 * W] = lo
-
-    def product(u, r):
-        full = jnp.dot(ds[pl.ds(r, RB), :], rhs[u], preferred_element_type=jnp.float32)
+            e = jnp.concatenate([land[u, a, k] for k in range(NY)], axis=0)
+            hi = e.astype(jnp.bfloat16)
+            lo = (e - hi.astype(jnp.float32)).astype(jnp.bfloat16)
+            r = a * NY * SHARD
+            for off in (0, K):
+                rhs[u, off + r:off + r + NY * SHARD, 0:W] = hi
+                rhs[u, off + r:off + r + NY * SHARD, W:2 * W] = lo
+
+    def product(u, r, n=RB):
+        full = jnp.dot(ds[pl.ds(r, n), :], rhs[u], preferred_element_type=jnp.float32)
         return full[:, 0:W] + full[:, W:2 * W]
 
-    for i in range(ROWS // DCH):
-        load(i).start()
-    for u in (2, 1, 3, 0):
-        own_piece(u).start()
+    def finish():
+        for copy in due.values():
+            copy.wait_recv()
+        for copy in sent:
+            copy.wait_send()
+
     barrier = pltpu.get_barrier_semaphore()
     for peer in [at_z(d) for d in ZS] + [at_y(d) for d in YS] + [at_x(d) for d in XS]:
         pl.semaphore_signal(barrier, inc=1, device_id=peer, device_id_type=MESH)
+    own_piece(2).start()
     pl.semaphore_wait(barrier, len(ZS) + len(YS) + len(XS))
-
     z_start(2)
+    for i in range(ROWS // DCH):
+        load(i).start()
+    for u in (1, 3, 0):
+        own_piece(u).start()
+    z_start(1)
+    z_start(3)
     for i in range(0, 4):
         split(i)
     y_start(2)
-    z_start(1)
-    z_start(3)
     for i in range(4, 8):
         split(i)
     for i in range(3):
-        sq_send(i).start()
+        go(sq_send, i)
     y_wait(2)
     panel(2)
 
     def far_block(b):
         for way, base in ((PLUS, HALF), (MINUS, 0)):
             out_x[FAR, way, pl.ds(b * RB, RB), :] = product(2, base + b * RB)
-            x_send(FAR, way, b).start()
+            go(x_send, FAR, way, b)
 
     for b in range(0, NB // 2):
         far_block(b)
@@ -157,26 +173,26 @@
     for b in range(NB):
         for way, base, u in ((PLUS, 0, 1), (MINUS, HALF, 3)):
             out_x[NEAR, way, pl.ds(b * RB, RB), :] = product(u, base + b * RB)
-            x_send(NEAR, way, b).start()
+            go(x_send, NEAR, way, b)
     y_start(0)
     for b in range(NB):
         for way, base, u in ((PLUS, HALF, 1), (MINUS, 0, 3)):
             mine = product(u, base + b * RB)
-            x_send(FAR, way, b).wait_recv()
+            got(x_send, FAR, way, b)
             out_x[SUM, way, pl.ds(b * RB, RB), :] = mine + in_x[FAR, way, pl.ds(b * RB, RB), :]
-            x_send(SUM, way, b).start()
+            go(x_send, SUM, way, b)
     y_wait(0)
     panel(0)
     for b in range(ROWS // RB):
         o_ref[pl.ds(b * RB, RB), :] = product(0, b * RB)
     for i in range(3):
-        sq_send(i).wait_recv()
+        got(sq_send, i)
     inverse = lax.rsqrt(sq[...] + sqin[0] + sqin[1] + sqin[2] + EPS)
     for b in range(NB):
-        x_send(NEAR, PLUS, b).wait_recv()
-        x_send(NEAR, MINUS, b).wait_recv()
+        got(x_send, NEAR, PLUS, b)
+        got(x_send, NEAR, MINUS, b)
         for way, base, near in ((PLUS, HALF, MINUS), (MINUS, 0, PLUS)):
-            x_send(SUM, way, b).wait_recv()
+            got(x_send, SUM, way, b)
             r = base + b * RB
             total = (o_ref[pl.ds(r, RB), :] + in_x[NEAR, near, pl.ds(b * RB, RB), :]
                      + in_x[SUM, way, pl.ds(b * RB, RB), :])
@@ -184,19 +200,7 @@
                 i = r // W + c
                 scale = jnp.broadcast_to(inverse[i:i + 1, :], (W, W)).T
                 o_ref[pl.ds(r + c * W, W), :] = total[c * W:(c + 1) * W] * scale
-
-    for u in range(NX):
-        for i in range(NZ - 1):
-            z_send(u, i).wait_send()
-        for i in range(NZ):
-            for j in range(3):
-                y_send(u, i, j).wait_send()
-    for i in range(3):
-        sq_send(i).wait_send()
-    for part in range(3):
-        for way in range(2):
-            for b in range(NB):
-                x_send(part, way, b).wait_send()
+    finish()
 
 
 def shards(decoder_slab, encoder_panel):
@@ -204,7 +208,7 @@
     dma = pltpu.SemaphoreType.DMA
     out = pl.pallas_call(
         kernel,
-        out_shape=jax.ShapeDtypeStruct((ROWS, W), f32),
+        out_shape=pltpu.VMEM((ROWS, W), f32),
         in_specs=[pl.BlockSpec(memory_space=pl.ANY)] * 2,
         out_specs=pl.BlockSpec(memory_space=pltpu.VMEM),
         scratch_shapes=[

time: 61 us -> 58.5 us (0.959)
  Pallas kernels: 58.8 us -> 57.5 us
  local copies, waits for them, and re-layouts: 2.05 us -> 0.97 us
    pallas_call x1, Pallas kernels: 58.8 us -> 57.5 us  [shards(): pl.pallas_call(kernel, out_shape=pltpu.VMEM((ROWS, W), f32), in_specs=[pl...]
    unnamed x1, local copies, waits for them, and re-layouts: 2.05 us -> 0.97 us
where the time goes in v2:
time: 58.5 us
  Pallas kernels  57.5 us (98%)
  local copies, waits for them, and re-layouts  0.97 us (2%)
    pallas_call x1, Pallas kernels, shards(): pl.pallas_call(kernel, out_shape=pltpu.VMEM((ROWS, W), f32), in_specs=[pl...  57.5 us

profile of v2, /device:TPU:2, one launch (start us, length us, event | category | flops | bytes accessed | tf_op | source)
XLA Modules:
  0.0 58.5 jit_solution(2697340482491729908)
XLA Ops:
  0.0 57.5 %shard_map.28 = f32[2048,128]{1,0:T(8,128)S(1)} custom-call(f32[2048,896]{1,0:T(8,128)} %d_ref.1, f32[28,512]{1,0:T(8,128)} %e_ref.1), custom_call_target="tpu_custom_call" | custom-call | tf_op jit(solution)/shard_map/pallas_call | solution.py:209
  57.5 1.0 %copy.5 = f32[2048,1,128]{2,1,0:T(1,128)} copy(f32[2048,1,128]{2,1,0:T(1,128)S(1)} %bitcast.3) | data formatting | bytes 2097152

commit v3 on v2

v3 whole, which is shorter than its diff:
```python
import jax
import jax.numpy as jnp
from jax import lax
from jax.experimental import pallas as pl
from jax.experimental.pallas import tpu as pltpu
from jax.sharding import PartitionSpec as P

EPS = 1e-06
MESH = pl.DeviceIdType.MESH
NX, NY, NZ = 4, 4, 8
ROWS, K, W = 2048, 896, 128
SHARD = K // (NY * NZ)
CARRY = 160
PIECE = CARRY // 4
KEPT = ROWS - CARRY
HALF = KEPT // 2
BLOCKS = ((0, 240), (240, 240), (480, 240), (720, 224))
NB = len(BLOCKS)
DCH = 256
ZS = (4, 3, 5, 2, 6, 1, 7)
YS = (2, 1, 3)
XS = (2, 1, 3)
UNIT = (2, 1, 3, 0)
GROUPS = ((0, 1), (1, 2), (3, 1), (4, 3))
FAR, NEAR, SUM = 0, 1, 2
PLUS, MINUS = 0, 1


def kernel(d_ref, e_ref, o_ref, dbuf, ds, land, rhs, sq, sqin, scale, out_x, in_x, car, cds,
           dsem, esem, pss, prs, zss, zrs, yss, yrs, wss, wrs, fss, frs, xss, xrs, qss, qrs, css, crs):
    h = lax.axis_index("hid")
    s = lax.axis_index("src")
    core = lax.axis_index("tgt")
    z, y = s // NY, lax.rem(s, NY)

    def at_x(d):
        return {"hid": lax.rem(h + d, NX)}

    def at_z(d):
        return {"src": lax.rem(z + d, NZ) * NY + y}

    def at_y(d):
        return {"src": z * NY + lax.rem(y + d, NY)}

    def remote(src, dst, send, recv, peer):
        return pltpu.make_async_remote_copy(
            src_ref=src, dst_ref=dst, send_sem=send, recv_sem=recv, device_id=peer, device_id_type=MESH)

    def load(i):
        return pltpu.make_async_copy(
            d_ref.at[pl.ds(i * DCH, DCH)], dbuf.at[pl.ds(i * DCH, DCH)], dsem.at[i])

    def columns(d):
        t = lax.rem(h + d, NX)
        return e_ref.at[:, pl.ds(pl.multiple_of(t * W, W), W)]

    def own_piece(u):
        return pltpu.make_async_copy(columns(UNIT[u]), land.at[u, z, y], esem.at[u])

    def piece_send(d):
        return remote(columns(d), land.at[7 - d, z, y], pss.at[d - 1], prs.at[d - 1], at_x(d))

    def z_send(g, i):
        if g == 0:
            src, dst = columns(UNIT[0]), land.at[0, z, y]
        else:
            src = dst = land.at[pl.ds(*GROUPS[g]), z, y]
        return remote(src, dst, zss.at[g, i], zrs.at[g, i], at_z(ZS[i]))

    def first_send(i, j):
        zz = z if i == NZ - 1 else lax.rem(z + NZ - ZS[i], NZ)
        return remote(land.at[0, zz, y], land.at[0, zz, y], yss.at[i, j], yrs.at[i, j], at_y(YS[j]))

    def column_send(g, way):
        part = land.at[pl.ds(*GROUPS[g]), :, y]
        return remote(part, part, wss.at[g, way], wrs.at[g, way], at_y(1 if way == PLUS else 3))

    def half_send(g, way):
        yy = lax.rem(y + (3 if way == PLUS else 1), NY)
        part = land.at[pl.ds(*GROUPS[g]), pl.ds(0 if way == PLUS else NZ // 2, NZ // 2), yy]
        return remote(part, part, fss.at[g, way], frs.at[g, way], at_y(1 if way == PLUS else 3))

    def sq_send(i):
        return remote(sq, sqin.at[i], qss.at[i], qrs.at[i], at_x(XS[i]))

    def x_send(part, way, b):
        rows = pl.ds(*BLOCKS[b])
        return remote(out_x.at[part, way, rows], in_x.at[part, way, rows], xss.at[part, way, b],
                      xrs.at[part, way, b], at_x(1 if way == PLUS else 3))

    def carry_send(way, p):
        r = pl.multiple_of(KEPT + core * (2 * PIECE) + p * PIECE, 8)
        return remote(d_ref.at[pl.ds(r, PIECE)], car.at[core, 2 if way == PLUS else 0, p],
                      css.at[way, p], crs.at[way, p], at_x(1 if way == PLUS else 3))

    def carry_on(way):
        p = 0 if way == PLUS else 1
        return remote(car.at[core, 2 if way == PLUS else 0, p], car.at[core, 1, p],
                      css.at[way, 2], crs.at[way, 2], at_x(1 if way == PLUS else 3))

    def carry_share():
        return remote(car.at[core], car.at[core], css.at[2, 0], crs.at[2, 0], {"tgt": 1 - core})

    def halves(d):
        hi = d.astype(jnp.bfloat16)
        return hi, (d - hi.astype(jnp.float32)).astype(jnp.bfloat16)

    def split(i):
        load(i).wait()
        d = dbuf[pl.ds(i * DCH, DCH), :]
        hi, lo = halves(d)
        ds[pl.ds(i * DCH, DCH), 0:K] = hi
        ds[pl.ds(i * DCH, DCH), K:2 * K] = lo
        p = d[:, 0:W] * d[:, 0:W]
        for c in range(1, K // W):
            q = d[:, c * W:(c + 1) * W]
            p = p + q * q
        for c in range(DCH // W):
            row = jnp.sum(p[c * W:(c + 1) * W].T, axis=0, keepdims=True)
            sq[i * (DCH // W) + c:i * (DCH // W) + c + 1, :] = row

    sent, due = [], {}

    def go(make, *key):
        copy = make(*key)
        copy.start()
        sent.append(copy)
        due[(make,) + key] = copy

    def got(make, *key):
        due.pop((make,) + key).wait_recv()

    def z_start(g):
        for i in range(NZ - 1):
            go(z_send, g, i)

    def z_wait(g):
        for i in range(NZ - 1):
            got(z_send, g, i)

    def columns_start(g):
        z_wait(g)
        for way in (PLUS, MINUS):
            go(column_send, g, way)

    def halves_start(g):
        for way in (PLUS, MINUS):
            got(column_send, g, way)
            go(half_send, g, way)

    def halves_wait(g):
        for way in (PLUS, MINUS):
            got(half_send, g, way)

    def panel(u):
        for a in range(NZ):
            e = jnp.concatenate([land[u, a, k] for k in range(NY)], axis=0)
            hi, lo = halves(e)
            r = a * NY * SHARD
            for off in (0, K):
                rhs[u, off + r:off + r + NY * SHARD, 0:W] = hi
                rhs[u, off + r:off + r + NY * SHARD, W:2 * W] = lo

    def dot(left, u):
        full = jnp.dot(left, rhs[u], preferred_element_type=jnp.float32)
        return full[:, 0:W] + full[:, W:2 * W]

    def product(u, r, n):
        return dot(ds[pl.ds(r, n), :], u)

    barrier = pltpu.get_barrier_semaphore()
    peers = [at_z(d) for d in ZS] + [at_y(d) for d in YS] + [at_x(d) for d in XS] + [{"tgt": 1 - core}]
    for peer in peers:
        pl.semaphore_signal(barrier, inc=1, device_id=peer, device_id_type=MESH)
    for u in range(NX):
        own_piece(u).start()
    pl.semaphore_wait(barrier, len(peers))

    z_start(0)
    for d in XS:
        go(piece_send, d)
    for p in (0, 1):
        go(carry_send, PLUS, p)
        go(carry_send, MINUS, 1 - p)
    for i in range(ROWS // DCH):
        load(i).start()
    for u in range(NX):
        own_piece(u).wait()
    z_start(1)
    for i in range(0, 4):
        split(i)
    for j in range(3):
        go(first_send, NZ - 1, j)
    for i in range(NZ - 1):
        got(z_send, 0, i)
        for j in range(3):
            go(first_send, i, j)
    got(carry_send, PLUS, 0)
    go(carry_on, PLUS)
    got(carry_send, MINUS, 1)
    go(carry_on, MINUS)
    for i in range(4, 8):
        split(i)
    for i in range(3):
        go(sq_send, i)
    for d in XS:
        got(piece_send, d)
    z_start(2)
    z_start(3)
    columns_start(1)
    for i in range(NZ):
        for j in range(3):
            got(first_send, i, j)
    panel(0)

    for b, (r, n) in enumerate(BLOCKS):
        for way, base in ((PLUS, HALF), (MINUS, 0)):
            out_x[FAR, way, pl.ds(r, n), :] = product(0, base + r, n)
            go(x_send, FAR, way, b)
    halves_start(1)
    columns_start(2)
    columns_start(3)
    halves_wait(1)
    panel(1)
    panel(2)
    for b, (r, n) in enumerate(BLOCKS):
        for way, base, u in ((PLUS, 0, 1), (MINUS, HALF, 2)):
            out_x[NEAR, way, pl.ds(r, n), :] = product(u, base + r, n)
            go(x_send, NEAR, way, b)
    for b, (r, n) in enumerate(BLOCKS):
        for way, base, u in ((PLUS, HALF, 1), (MINUS, 0, 2)):
            mine = product(u, base + r, n)
            got(x_send, FAR, way, b)
            out_x[SUM, way, pl.ds(r, n), :] = mine + in_x[FAR, way, pl.ds(r, n), :]
            go(x_send, SUM, way, b)

    got(carry_send, PLUS, 1)
    got(carry_send, MINUS, 0)
    got(carry_on, PLUS)
    got(carry_on, MINUS)
    go(carry_share)
    halves_start(2)
    halves_start(3)
    for i in range(3):
        got(sq_send, i)
    inverse = lax.rsqrt(sq[...] + sqin[0] + sqin[1] + sqin[2] + EPS)
    for i in range(ROWS // W):
        scale[i * W:(i + 1) * W, :] = jnp.broadcast_to(inverse[i:i + 1, :], (W, W)).T
    got(carry_share)
    for k in range(3):
        for c in range(2):
            d = jnp.concatenate([car[c, k, 0], car[c, k, 1]], axis=0)
            hi, lo = halves(d)
            cds[k, c * 2 * PIECE:(c + 1) * 2 * PIECE, 0:K] = hi
            cds[k, c * 2 * PIECE:(c + 1) * 2 * PIECE, K:2 * K] = lo
    halves_wait(2)
    panel(3)
    for r, n in [(r, 256) for r in range(0, ROWS, 256)]:
        o_ref[pl.ds(r, n), :] = product(3, r, n)
    halves_wait(3)
    for u in (4, 5, 6):
        panel(u)
    total = o_ref[KEPT:ROWS, :]
    for k in range(3):
        total = total + dot(cds[k], 4 + k)
    o_ref[KEPT:ROWS, :] = total * scale[KEPT:ROWS, :]

    for b, (r, n) in enumerate(BLOCKS):
        got(x_send, NEAR, PLUS, b)
        got(x_send, NEAR, MINUS, b)
        for way, base, near in ((PLUS, HALF, MINUS), (MINUS, 0, PLUS)):
            got(x_send, SUM, way, b)
            rows = pl.ds(base + r, n)
            o_ref[rows, :] = (o_ref[rows, :] + in_x[NEAR, near, pl.ds(r, n), :]
                              + in_x[SUM, way, pl.ds(r, n), :]) * scale[rows, :]

    for copy in due.values():
        copy.wait_recv()
    for copy in sent:
        copy.wait_send()


def shards(decoder_slab, encoder_panel):
    f32, bf16 = jnp.float32, jnp.bfloat16
    dma = pltpu.SemaphoreType.DMA
    ng = len(GROUPS)
    out = pl.pallas_call(
        kernel,
        out_shape=pltpu.VMEM((ROWS, W), f32),
        in_specs=[pl.BlockSpec(memory_space=pl.ANY)] * 2,
        out_specs=pl.BlockSpec(memory_space=pltpu.VMEM),
        scratch_shapes=[
            pltpu.VMEM((ROWS, K), f32),
            pltpu.VMEM((ROWS, 2 * K), bf16),
            pltpu.VMEM((7, NZ, NY, SHARD, W), f32),
            pltpu.VMEM((7, 2 * K, 2 * W), bf16),
            pltpu.VMEM((ROWS // W, W), f32),
            pltpu.VMEM((3, ROWS // W, W), f32),
            pltpu.VMEM((ROWS, W), f32),
            pltpu.VMEM((3, 2, HALF, W), f32),
            pltpu.VMEM((3, 2, HALF, W), f32),
            pltpu.VMEM((2, 3, 2, PIECE, K), f32),
            pltpu.VMEM((3, CARRY, 2 * K), bf16),
            dma((ROWS // DCH,)), dma((NX,)),
            dma((3,)), dma((3,)),
            dma((ng, NZ - 1)), dma((ng, NZ - 1)),
            dma((NZ, 3)), dma((NZ, 3)),
            dma((ng, 2)), dma((ng, 2)),
            dma((ng, 2)), dma((ng, 2)),
            dma((3, 2, NB)), dma((3, 2, NB)),
            dma((3,)), dma((3,)),
            dma((3, 3)), dma((3, 3)),
        ],
        compiler_params=pltpu.CompilerParams(
            collective_id=0, has_side_effects=True, vmem_limit_bytes=56 * 1024 * 1024),
    )(decoder_slab, encoder_panel)
    return out.reshape(ROWS, 1, W)


def solution(mesh):
    placed = (P("src", "hid"), P(("hid", "src"), "tgt"))
    return jax.shard_map(
        shards, mesh=mesh, in_specs=placed, out_specs=P("src", "tgt", "hid"), check_vma=False
    )
```

time: 58.5 us -> 55.1 us (0.942); the launches traced: 58.5 us -> 54.4 us
  Pallas kernels: 57.5 us -> 53.4 us
    pallas_call x1, Pallas kernels: 57.5 us -> 53.4 us  [shards(): pl.pallas_call(kernel, out_shape=pltpu.VMEM((ROWS, W), f32), in_specs=[pl...]
where the time goes in v3:
time: 55.1 us; the launch traced here: 54.4 us
  Pallas kernels  53.4 us (97%)
  local copies, waits for them, and re-layouts  0.97 us (2%)
    pallas_call x1, Pallas kernels, shards(): pl.pallas_call(kernel, out_shape=pltpu.VMEM((ROWS, W), f32), in_specs=[pl...  53.4 us

profile of v3, /device:TPU:2, one launch (start us, length us, event | category | flops | bytes accessed | tf_op | source)
XLA Modules:
  0.0 54.4 jit_solution(12415661631958674539)
XLA Ops:
  0.0 53.4 %shard_map.28 = f32[2048,128]{1,0:T(8,128)S(1)} custom-call(f32[2048,896]{1,0:T(8,128)} %d_ref.1, f32[28,512]{1,0:T(8,128)} %e_ref.1), custom_call_target="tpu_custom_call" | custom-call | tf_op jit(solution)/shard_map/pallas_call | solution.py:287
  53.4 1.0 %copy.5 = f32[2048,1,128]{2,1,0:T(1,128)} copy(f32[2048,1,128]{2,1,0:T(1,128)S(1)} %bitcast.3) | data formatting | bytes 2097152

commit v4 on v3

v4 whole, which is shorter than its diff:
```python
import jax
import jax.numpy as jnp
from jax import lax
from jax.experimental import pallas as pl
from jax.experimental.pallas import tpu as pltpu
from jax.sharding import PartitionSpec as P

EPS = 1e-06
MESH = pl.DeviceIdType.MESH
NX, NY, NZ = 4, 4, 8
ROWS, K, W = 2048, 896, 128
SHARD = K // (NY * NZ)
PAIR = 256
PART = PAIR // 2
KEPT = ROWS - 2 * PAIR
HALF = KEPT // 2
BLOCKS = ((0, 128), (128, 256), (384, 256), (640, 128))
NB = len(BLOCKS)
DCH = 256
ZS = (1, 7, 2, 6, 3, 5, 4)
YS = (2, 1, 3)
XS = (2, 1, 3)
OWN = {0: 2, 1: 1, 2: 3, 5: 0}
PIECES = ((4, 2, 1), (3, 2, 3), (7, 1, 1), (6, 3, 3))
GROUPS = ((0, 1), (1, 1), (2, 1), (3, 2), (5, 2), (7, 1))
Y_FIRST = (2, 5)
FAR, NEAR, SUM = 0, 1, 2
PLUS, MINUS = 0, 1


def kernel(d_ref, e_ref, o_ref, dbuf, ds, land, rhs, sq, sqin, scale, out_x, in_x, out_p, in_p, car, cds,
           dsem, esem, pss, prs, zss, zrs, yss, yrs, uss, urs, vss, vrs, wss, wrs, fss, frs, xss, xrs, qss, qrs, css, crs, ass, ars):
    h = lax.axis_index("hid")
    s = lax.axis_index("src")
    core = lax.axis_index("tgt")
    z, y = s // NY, lax.rem(s, NY)
    odd = lax.rem(h, 2)
    pairs = (KEPT + odd * PAIR, KEPT + (1 - odd) * PAIR)

    def at_x(d):
        return {"hid": lax.rem(h + d, NX)}

    def at_z(d):
        return {"src": lax.rem(z + d, NZ) * NY + y}

    def at_y(d):
        return {"src": z * NY + lax.rem(y + d, NY)}

    def remote(src, dst, send, recv, peer):
        return pltpu.make_async_remote_copy(
            src_ref=src, dst_ref=dst, send_sem=send, recv_sem=recv, device_id=peer, device_id_type=MESH)

    def load(i):
        return pltpu.make_async_copy(
            d_ref.at[pl.ds(i * DCH, DCH)], dbuf.at[pl.ds(i * DCH, DCH)], dsem.at[i])

    def columns(d):
        t = lax.rem(h + d, NX)
        return e_ref.at[:, pl.ds(pl.multiple_of(t * W, W), W)]

    def own_piece(u):
        return pltpu.make_async_copy(columns(OWN[u]), land.at[u, z, y], esem.at[u])

    def piece_send(i):
        unit, d, peer = PIECES[i]
        return remote(columns(d), land.at[unit, z, y], pss.at[i], prs.at[i], at_x(peer))

    def z_send(i):
        return remote(columns(OWN[0]), land.at[0, z, y], zss.at[i], zrs.at[i], at_z(ZS[i]))

    def bundle(g, zz):
        return land.at[pl.ds(*GROUPS[g]), zz] if g in Y_FIRST else land.at[pl.ds(*GROUPS[g]), zz, y]

    def near_send(g, i):
        part = bundle(g, z)
        return remote(part, part, uss.at[g, i], urs.at[g, i], at_z((2, 6, 1, 7)[i]))

    def on_send(g, i):
        came, to = ((6, 1), (2, 7), (6 + 4 * core, 2 + 4 * core))[i]
        part = bundle(g, lax.rem(z + came, NZ))
        return remote(part, part, vss.at[g, i], vrs.at[g, i], at_z(to))

    def row_send(g, j):
        part = land.at[pl.ds(*GROUPS[g]), z, y]
        return remote(part, part, wss.at[g, j], wrs.at[g, j], at_y(YS[j]))

    def first_send(i, j):
        zz = z if i == NZ - 1 else lax.rem(z + NZ - ZS[i], NZ)
        return remote(land.at[0, zz, y], land.at[0, zz, y], yss.at[i, j], yrs.at[i, j], at_y(YS[j]))

    def column_send(g, way):
        part = land.at[pl.ds(*GROUPS[g]), :, y]
        return remote(part, part, wss.at[g, way], wrs.at[g, way], at_y(1 if way == PLUS else 3))

    def half_send(g, way):
        yy = lax.rem(y + (3 if way == PLUS else 1), NY)
        part = land.at[pl.ds(*GROUPS[g]), pl.ds(0 if way == PLUS else NZ // 2, NZ // 2), yy]
        return remote(part, part, fss.at[g, way], frs.at[g, way], at_y(1 if way == PLUS else 3))

    def sq_send(i):
        return remote(sq, sqin.at[i], qss.at[i], qrs.at[i], at_x(XS[i]))

    def x_send(part, way, b):
        rows = pl.ds(*BLOCKS[b])
        return remote(out_x.at[part, way, rows], in_x.at[part, way, rows], xss.at[part, way, b],
                      xrs.at[part, way, b], at_x(1 if way == PLUS else 3))

    def pair_send(way):
        r = pl.multiple_of(pairs[way] + core * PART, 16)
        return remote(d_ref.at[pl.ds(r, PART)], car.at[core, 1 - way], css.at[way], crs.at[way],
                      at_x(1 if way == PLUS else 3))

    def pair_share():
        return remote(car.at[core], car.at[core], css.at[2], crs.at[2], {"tgt": 1 - core})

    def pair_sum_send(way):
        return remote(out_p.at[way], in_p.at[way], ass.at[way], ars.at[way], at_x(1 if way == PLUS else 3))

    def pair_rows(which):
        return pl.ds(pl.multiple_of(pairs[which], 16), PAIR)

    def halves(d):
        hi = d.astype(jnp.bfloat16)
        return hi, (d - hi.astype(jnp.float32)).astype(jnp.bfloat16)

    def split(i):
        load(i).wait()
        d = dbuf[pl.ds(i * DCH, DCH), :]
        hi, lo = halves(d)
        ds[pl.ds(i * DCH, DCH), 0:K] = hi
        ds[pl.ds(i * DCH, DCH), K:2 * K] = lo
        p = d[:, 0:W] * d[:, 0:W]
        for c in range(1, K // W):
            q = d[:, c * W:(c + 1) * W]
            p = p + q * q
        for c in range(DCH // W):
            row = jnp.sum(p[c * W:(c + 1) * W].T, axis=0, keepdims=True)
            sq[i * (DCH // W) + c:i * (DCH // W) + c + 1, :] = row

    sent, due = [], {}

    def go(make, *key):
        copy = make(*key)
        copy.start()
        sent.append(copy)
        due[(make,) + key] = copy

    def got(make, *key):
        due.pop((make,) + key).wait_recv()

    def near_start(g):
        if g in Y_FIRST:
            for j in range(3):
                got(row_send, g, j)
        for i in range(4):
            go(near_send, g, i)

    def on_start(g):
        for i in range(4):
            got(near_send, g, i)
        for i in range(3):
            go(on_send, g, i)

    def on_wait(g):
        for i in range(3):
            got(on_send, g, i)

    def rows_start(g):
        for j in range(3):
            go(row_send, g, j)

    def columns_start(g):
        on_wait(g)
        for way in (PLUS, MINUS):
            go(column_send, g, way)

    def halves_start(g):
        for way in (PLUS, MINUS):
            got(column_send, g, way)
            go(half_send, g, way)

    def halves_wait(g):
        for way in (PLUS, MINUS):
            got(half_send, g, way)

    def panel_part(u, a):
        hi, lo = halves(jnp.concatenate([land[u, a, k] for k in range(NY)], axis=0))
        for off in (0, K):
            rows = pl.ds(pl.multiple_of(off + a * (NY * SHARD), 16), NY * SHARD)
            rhs[u, rows, 0:W] = hi
            rhs[u, rows, W:2 * W] = lo

    def panel(u):
        for a in range(NZ):
            panel_part(u, a)

    def dot(left, u):
        full = jnp.dot(left, rhs[u], preferred_element_type=jnp.float32)
        return full[:, 0:W] + full[:, W:2 * W]

    def product(u, r, n):
        return dot(ds[pl.ds(r, n), :], u)

    barrier = pltpu.get_barrier_semaphore()
    peers = [at_z(d) for d in ZS] + [at_y(d) for d in YS] + [at_x(d) for d in XS] + [{"tgt": 1 - core}]
    for peer in peers:
        pl.semaphore_signal(barrier, inc=1, device_id=peer, device_id_type=MESH)
    for u in OWN:
        own_piece(u).start()
    pl.semaphore_wait(barrier, len(peers))

    for i in range(NZ - 1):
        go(z_send, i)
    for i in range(len(PIECES)):
        go(piece_send, i)
    for way in (PLUS, MINUS):
        go(pair_send, way)
    for u in OWN:
        own_piece(u).wait()
    rows_start(2)
    for j in range(3):
        go(first_send, NZ - 1, j)
    near_start(1)
    for i in range(ROWS // DCH):
        load(i).start()
    for i in range(0, 4):
        split(i)
    for i in range(NZ - 1):
        got(z_send, i)
        for j in range(3):
            go(first_send, i, j)
        if i == 3:
            near_start(2)
        if i == 5:
            on_start(1)
    for i in range(len(PIECES)):
        got(piece_send, i)
    near_start(3)
    near_start(4)
    rows_start(5)
    for i in range(4, 8):
        split(i)
    for i in range(3):
        go(sq_send, i)
    columns_start(1)
    for i in (NZ - 1,) + tuple(range(NZ - 1)):
        for j in range(3):
            got(first_send, i, j)
        panel_part(0, z if i == NZ - 1 else lax.rem(z + NZ - ZS[i], NZ))

    for b, (r, n) in enumerate(BLOCKS):
        for way, base in ((PLUS, HALF), (MINUS, 0)):
            out_x[FAR, way, pl.ds(r, n), :] = product(0, base + r, n)
            go(x_send, FAR, way, b)
        if b == 0:
            on_start(2)
    on_start(3)
    on_start(4)
    halves_start(1)
    halves_wait(1)
    panel(1)
    on_wait(2)
    panel(2)
    for b, (r, n) in enumerate(BLOCKS):
        for way, base, u in ((PLUS, 0, 1), (MINUS, HALF, 2)):
            out_x[NEAR, way, pl.ds(r, n), :] = product(u, base + r, n)
            go(x_send, NEAR, way, b)
        if b == 1:
            columns_start(3)
            near_start(5)
            columns_start(4)
    for way in (PLUS, MINUS):
        got(pair_send, way)
    go(pair_share)
    halves_start(3)
    on_start(5)
    for b, (r, n) in enumerate(BLOCKS):
        for way, base, u in ((PLUS, HALF, 1), (MINUS, 0, 2)):
            mine = product(u, base + r, n)
            got(x_send, FAR, way, b)
            out_x[SUM, way, pl.ds(r, n), :] = mine + in_x[FAR, way, pl.ds(r, n), :]
            go(x_send, SUM, way, b)

    got(pair_share)
    for which in range(2):
        for c in range(2):
            hi, lo = halves(car[c, which])
            cds[which, c * PART:(c + 1) * PART, 0:K] = hi
            cds[which, c * PART:(c + 1) * PART, K:2 * K] = lo
    halves_start(4)
    halves_wait(3)
    panel(3)
    panel(4)
    for way, which, mine, theirs in ((PLUS, 1, 1, 4), (MINUS, 0, 2, 3)):
        out_p[way] = dot(ds[pair_rows(which), :], mine) + dot(cds[which], theirs)
        go(pair_sum_send, way)
    for i in range(3):
        got(sq_send, i)
    inverse = lax.rsqrt(sq[...] + sqin[0] + sqin[1] + sqin[2] + EPS)
    for i in range(ROWS // W):
        scale[i * W:(i + 1) * W, :] = jnp.broadcast_to(inverse[i:i + 1, :], (W, W)).T
    halves_wait(4)
    on_wait(5)
    for u in (5, 6, 7):
        panel(u)
    for r in range(0, KEPT, 256):
        n = min(256, KEPT - r)
        o_ref[pl.ds(r, n), :] = product(5, r, n)
    for which in range(2):
        o_ref[pair_rows(which), :] = dot(ds[pair_rows(which), :], 5) + dot(cds[which], 6 + which)

    for b, (r, n) in enumerate(BLOCKS):
        got(x_send, NEAR, PLUS, b)
        got(x_send, NEAR, MINUS, b)
        for way, base, near in ((PLUS, HALF, MINUS), (MINUS, 0, PLUS)):
            got(x_send, SUM, way, b)
            rows = pl.ds(base + r, n)
            o_ref[rows, :] = (o_ref[rows, :] + in_x[NEAR, near, pl.ds(r, n), :]
                              + in_x[SUM, way, pl.ds(r, n), :]) * scale[rows, :]
    for way, which in ((PLUS, 0), (MINUS, 1)):
        got(pair_sum_send, way)
        rows = pair_rows(which)
        o_ref[rows, :] = (o_ref[rows, :] + in_p[way]) * scale[rows, :]

    for copy in due.values():
        copy.wait_recv()
    for copy in sent:
        copy.wait_send()


def shards(decoder_slab, encoder_panel):
    f32, bf16 = jnp.float32, jnp.bfloat16
    dma = pltpu.SemaphoreType.DMA
    ng = len(GROUPS)
    out = pl.pallas_call(
        kernel,
        out_shape=pltpu.VMEM((ROWS, W), f32),
        in_specs=[pl.BlockSpec(memory_space=pl.ANY)] * 2,
        out_specs=pl.BlockSpec(memory_space=pltpu.VMEM),
        scratch_shapes=[
            pltpu.VMEM((ROWS, K), f32),
            pltpu.VMEM((ROWS, 2 * K), bf16),
            pltpu.VMEM((8, NZ, NY, SHARD, W), f32),
            pltpu.VMEM((8, 2 * K, 2 * W), bf16),
            pltpu.VMEM((ROWS // W, W), f32),
            pltpu.VMEM((3, ROWS // W, W), f32),
            pltpu.VMEM((ROWS, W), f32),
            pltpu.VMEM((3, 2, HALF, W), f32),
            pltpu.VMEM((3, 2, HALF, W), f32),
            pltpu.VMEM((2, PAIR, W), f32),
            pltpu.VMEM((2, PAIR, W), f32),
            pltpu.VMEM((2, 2, PART, K), f32),
            pltpu.VMEM((2, PAIR, 2 * K), bf16),
            dma((ROWS // DCH,)), dma((8,)),
            dma((len(PIECES),)), dma((len(PIECES),)),
            dma((NZ - 1,)), dma((NZ - 1,)),
            dma((NZ, 3)), dma((NZ, 3)),
            dma((ng, 4)), dma((ng, 4)),
            dma((ng, 3)), dma((ng, 3)),
            dma((ng, 3)), dma((ng, 3)),
            dma((ng, 2)), dma((ng, 2)),
            dma((3, 2, NB)), dma((3, 2, NB)),
            dma((3,)), dma((3,)),
            dma((3,)), dma((3,)),
            dma((2,)), dma((2,)),
        ],
        compiler_params=pltpu.CompilerParams(
            collective_id=0, has_side_effects=True, vmem_limit_bytes=56 * 1024 * 1024),
    )(decoder_slab, encoder_panel)
    return out.reshape(ROWS, 1, W)


def solution(mesh):
    placed = (P("src", "hid"), P(("hid", "src"), "tgt"))
    return jax.shard_map(
        shards, mesh=mesh, in_specs=placed, out_specs=P("src", "tgt", "hid"), check_vma=False
    )
```

time: 55.1 us -> 54.1 us (0.982); the launches traced: 54.4 us -> 54.1 us
  no operation moved by 1% of the time
where the time goes in v4:
time: 54.1 us
  Pallas kernels  53.1 us (98%)
  local copies, waits for them, and re-layouts  0.97 us (2%)
    pallas_call x1, Pallas kernels, shards(): pl.pallas_call(kernel, out_shape=pltpu.VMEM((ROWS, W), f32), in_specs=[pl...  53.1 us

profile of v4, /device:TPU:2, one launch (start us, length us, event | category | flops | bytes accessed | tf_op | source)
XLA Modules:
  0.0 54.1 jit_solution(13995203591268307600)
XLA Ops:
  0.0 53.1 %shard_map.28 = f32[2048,128]{1,0:T(8,128)S(1)} custom-call(f32[2048,896]{1,0:T(8,128)} %d_ref.1, f32[28,512]{1,0:T(8,128)} %e_ref.1), custom_call_target="tpu_custom_call" | custom-call | tf_op jit(solution)/shard_map/pallas_call | solution.py:335
  53.1 1.0 %copy.5 = f32[2048,1,128]{2,1,0:T(1,128)} copy(f32[2048,1,128]{2,1,0:T(1,128)S(1)} %bitcast.3) | data formatting | bytes 2097152

commit v5 on v4

--- a/solution.py
+++ b/solution.py
@@ -10,11 +10,11 @@
 NX, NY, NZ = 4, 4, 8
 ROWS, K, W = 2048, 896, 128
 SHARD = K // (NY * NZ)
-PAIR = 256
+PAIR = 224
 PART = PAIR // 2
 KEPT = ROWS - 2 * PAIR
 HALF = KEPT // 2
-BLOCKS = ((0, 128), (128, 256), (384, 256), (640, 128))
+BLOCKS = ((0, 128), (128, 272), (400, 272), (672, 128))
 NB = len(BLOCKS)
 DCH = 256
 ZS = (1, 7, 2, 6, 3, 5, 4)
@@ -242,7 +242,6 @@
         split(i)
     for i in range(3):
         go(sq_send, i)
-    columns_start(1)
     for i in (NZ - 1,) + tuple(range(NZ - 1)):
         for j in range(3):
             got(first_send, i, j)
@@ -253,6 +252,7 @@
             out_x[FAR, way, pl.ds(r, n), :] = product(0, base + r, n)
             go(x_send, FAR, way, b)
         if b == 0:
+            columns_start(1)
             on_start(2)
     on_start(3)
     on_start(4)

time: 54.1 us -> 53.7 us (level)
  no operation moved by 1% of the time
where the time goes in v5:
time: 53.7 us; the launch traced here: 53.6 us
  Pallas kernels  52.7 us (98%)
  local copies, waits for them, and re-layouts  0.97 us (2%)
    pallas_call x1, Pallas kernels, shards(): pl.pallas_call(kernel, out_shape=pltpu.VMEM((ROWS, W), f32), in_specs=[pl...  52.7 us

profile of v5, /device:TPU:2, one launch (start us, length us, event | category | flops | bytes accessed | tf_op | source)
XLA Modules:
  0.0 53.6 jit_solution(13074221541551720780)
XLA Ops:
  0.0 52.7 %shard_map.28 = f32[2048,128]{1,0:T(8,128)S(1)} custom-call(f32[2048,896]{1,0:T(8,128)} %d_ref.1, f32[28,512]{1,0:T(8,128)} %e_ref.1), custom_call_target="tpu_custom_call" | custom-call | tf_op jit(solution)/shard_map/pallas_call | solution.py:335
  52.7 1.0 %copy.5 = f32[2048,1,128]{2,1,0:T(1,128)} copy(f32[2048,1,128]{2,1,0:T(1,128)S(1)} %bitcast.3) | data formatting | bytes 2097152

commit v6 on v5

--- a/solution.py
+++ b/solution.py
@@ -300,13 +300,13 @@
     for i in range(ROWS // W):
         scale[i * W:(i + 1) * W, :] = jnp.broadcast_to(inverse[i:i + 1, :], (W, W)).T
     halves_wait(4)
-    on_wait(5)
-    for u in (5, 6, 7):
-        panel(u)
+    panel(5)
     for r in range(0, KEPT, 256):
         n = min(256, KEPT - r)
         o_ref[pl.ds(r, n), :] = product(5, r, n)
+    on_wait(5)
     for which in range(2):
+        panel(6 + which)
         o_ref[pair_rows(which), :] = dot(ds[pair_rows(which), :], 5) + dot(cds[which], 6 + which)
 
     for b, (r, n) in enumerate(BLOCKS):

time: 53.7 us -> 54 us (level)
  no operation moved by 1% of the time
where the time goes in v6:
time: 54 us; the launch traced here: 53.9 us
  Pallas kernels  52.9 us (98%)
  local copies, waits for them, and re-layouts  0.97 us (2%)
    pallas_call x1, Pallas kernels, shards(): pl.pallas_call(kernel, out_shape=pltpu.VMEM((ROWS, W), f32), in_specs=[pl...  52.9 us

profile of v6, /device:TPU:2, one launch (start us, length us, event | category | flops | bytes accessed | tf_op | source)
XLA Modules:
  0.0 53.9 jit_solution(18164030611300463434)
XLA Ops:
  0.0 52.9 %shard_map.28 = f32[2048,128]{1,0:T(8,128)S(1)} custom-call(f32[2048,896]{1,0:T(8,128)} %d_ref.1, f32[28,512]{1,0:T(8,128)} %e_ref.1), custom_call_target="tpu_custom_call" | custom-call | tf_op jit(solution)/shard_map/pallas_call | solution.py:335
  52.9 1.0 %copy.5 = f32[2048,1,128]{2,1,0:T(1,128)} copy(f32[2048,1,128]{2,1,0:T(1,128)S(1)} %bitcast.3) | data formatting | bytes 2097152
